TPU v7x, 256 devices: a whole 4x4x8 slice. The times are simulated.
256 devices in a mesh: item: 32 (over x_hi, z, core), sub: 8 (over x_lo, y).
Axes of the slice: x: 4 (x_hi: 2, x_lo: 2; x = x_hi * 2 + x_lo), y: 4, z: 8, core: 2. Of those that a mesh axis runs over, the one named last changes fastest.
Arguments:
- samples: bfloat16 [65536, 1024], P(('item', 'sub')), may hold values from -28 to 28
- rotation: bfloat16 [1024, 1024], replicated, may hold values from -0.1875 to 0.1875
- codebook: bfloat16 [8, 4096, 128], P('sub'), may hold values from -4 to 4
Outputs:
- codewords_new: float32 [8, 4096, 128], P('sub', 'item')
- cross_cov: float32 [1024, 1024], P('item', 'sub')
All inputs are finite; a program needn't handle non-finite values.
Results may differ from a plain program's by a relative error of at most 0.011.
Values may be sent and summed in bfloat16 or wider, within the bound.
A program may use at most 64 MiB of HBM per device.

v0:
```python
import math

import jax
import jax.numpy as jnp
from jax import lax
from jax.sharding import PartitionSpec as P


def assign_subspace(rotated_sub, codewords):
    sub_width = codewords.shape[1]
    code_count = codewords.shape[0]
    code_f = codewords.astype(jnp.float32)
    sqnorm = jnp.sum(code_f * code_f, axis=1)
    sharpness = 3.0 / math.sqrt(sub_width)
    total_rows = rotated_sub.shape[0]
    block_rows = math.gcd(total_rows, 512)
    blocks = rotated_sub.reshape(total_rows // block_rows, block_rows, sub_width)

    def step(carry, block):
        counts, totals = carry
        logits = (
            jnp.dot(block, codewords.T, preferred_element_type=jnp.float32) - 0.5 * sqnorm[None, :]
        ) * sharpness
        weights = jax.nn.softmax(logits, axis=1).astype(jnp.bfloat16)
        counts = counts + jnp.sum(weights.astype(jnp.float32), axis=0)
        totals = totals + jnp.dot(weights.T, block, preferred_element_type=jnp.float32)
        rebuilt = jnp.dot(weights, codewords, preferred_element_type=jnp.float32).astype(
            jnp.bfloat16
        )
        return ((counts, totals), rebuilt)

    init = (jnp.zeros((code_count,), jnp.float32), jnp.zeros((code_count, sub_width), jnp.float32))
    (counts, totals), rebuilt = lax.scan(step, init, blocks)
    return (counts, totals, rebuilt.reshape(total_rows, sub_width))


def body(samples, rotation, codebook):
    rotated = jnp.dot(samples, rotation, preferred_element_type=jnp.float32).astype(jnp.bfloat16)
    local_rows = lax.all_to_all(rotated, "sub", split_axis=1, concat_axis=0, tiled=True)
    counts, totals, rebuilt = assign_subspace(local_rows, codebook[0])
    count_list = [counts]
    total_list = [totals]
    all_counts = jnp.stack(count_list, axis=0)
    all_totals = jnp.stack(total_list, axis=0)
    share_totals, share_counts = (
        lax.psum_scatter(all_totals, "item", scatter_dimension=1, tiled=True),
        lax.psum_scatter(all_counts, "item", scatter_dimension=1, tiled=True),
    )
    share_size = share_counts.shape[1]
    old_share = lax.dynamic_slice_in_dim(
        codebook, lax.axis_index("item") * share_size, share_size, 1
    ).astype(jnp.float32)
    codewords_new = (share_totals + old_share) / (share_counts + 1.0)[:, :, None]
    rebuilt_rows = lax.all_to_all(rebuilt, "sub", split_axis=0, concat_axis=1, tiled=True)
    partial_cov = jnp.einsum("rd,re->de", samples, rebuilt_rows, preferred_element_type=jnp.float32)
    item_cov = lax.psum_scatter(partial_cov, "item", scatter_dimension=0, tiled=True)
    cross_cov = lax.psum_scatter(item_cov, "sub", scatter_dimension=1, tiled=True)
    return (codewords_new, cross_cov)


def solution(mesh):
    placed = (P(("item", "sub"), None), P(), P("sub", None, None))
    return jax.shard_map(
        body,
        mesh=mesh,
        in_specs=placed,
        out_specs=(P("sub", "item", None), P("item", "sub")),
        check_vma=False,
    )
```

profile of v0, /device:TPU:8, one launch (start us, length us, event | category | flops | bytes accessed | tf_op | source)
XLA Modules:
  0.0 531.3 jit_solution(1622119575391232374)
XLA Ops:
  11.5 6.2 %all-to-all-start = ((bf16[256,8,128]{2,0,1:T(8,128)(2,1)}), bf16[256,8,128]{2,0,1:T(8,128)(2,1)}, u32[]{:S(2)}, u32[]{:S(2)}) async-start(bf16[256,8,128]{2,0,1:T(8,128)(2,1)} %bitcast.61), calls=%async_computation | async-start | bytes 1048576 | tf_op jit(solution)/shard_map/all_to_all | solution.py:39
  18.4 7.1 %all-to-all-done = bf16[256,8,128]{2,0,1:T(8,128)(2,1)} async-done(((bf16[256,8,128]{2,0,1:T(8,128)(2,1)}), bf16[256,8,128]{2,0,1:T(8,128)(2,1)}, u32[]{:S(2)}, u32[]{:S(2)}) %all-to-all-start) | async-done | bytes 524320 | tf_op jit(solution)/shard_map/all_to_all | solution.py:39
  25.5 62.2 %while.15 = (s32[]{:T(128)}, f32[4096]{0:T(1024)S(1)}, f32[4096,128]{1,0:T(8,128)}, bf16[4,512,128]{2,1,0:T(8,128)(2,1)}, bf16[4,512,128]{2,1,0:T(8,128)(2,1)}, ...) while((s32[]{:T(128)}, f32[4096]{0:T(1024)S(1)}, ...), condition=%wide.region_5.6_spmd.clone, body=%wide.region_1.5_spmd.clone.sunk | while | flops 1641094144 | bytes 61369984 | solution.py:33
  25.5 2.3 fusion.33
  29.8 3.8 convert_reduce_fusion.2
  33.6 5.0 convolution_add_fusion.2
  40.5 2.3 fusion.33
  42.8 2.0 fusion.34
  44.8 3.8 convert_reduce_fusion.2
  48.6 5.7 %convolution_add_fusion.2 = f32[4096,128]{1,0:T(8,128)} fusion(bf16[512,4096]{1,0:T(8,128)(2,1)} %get-tuple-element.144, f32[4096,128]{1,0:T(8,128)} %get-tuple-element.156, pred[]{:T(512)S(6)} %compare.3, bf16[4,512,128]{2,1,0:T(8,128)(2,1)} %get-tuple-element.167, s32[]{:T(128)} %get-tuple-element.154), kind=kOutput, calls=%fused_computation.6.clone.1 | convolution fusion | flops 537919488 | bytes 8520193 | tf_op jit(solution)/shard_map/while/body/eval_jaxpr/dot_general | solution.py:26
  56.2 2.3 fusion.33
  60.5 3.8 convert_reduce_fusion.2
  64.3 5.7 %convolution_add_fusion.2 = f32[4096,128]{1,0:T(8,128)} fusion(bf16[512,4096]{1,0:T(8,128)(2,1)} %get-tuple-element.144, f32[4096,128]{1,0:T(8,128)} %get-tuple-element.156, pred[]{:T(512)S(6)} %compare.3, bf16[4,512,128]{2,1,0:T(8,128)(2,1)} %get-tuple-element.167, s32[]{:T(128)} %get-tuple-element.154), kind=kOutput, calls=%fused_computation.6.clone.1 | convolution fusion | flops 537919488 | bytes 8520193 | tf_op jit(solution)/shard_map/while/body/eval_jaxpr/dot_general | solution.py:26
  72.0 2.3 fusion.33
  76.3 3.8 convert_reduce_fusion.2
  80.0 5.7 %convolution_add_fusion.2 = f32[4096,128]{1,0:T(8,128)} fusion(bf16[512,4096]{1,0:T(8,128)(2,1)} %get-tuple-element.144, f32[4096,128]{1,0:T(8,128)} %get-tuple-element.156, pred[]{:T(512)S(6)} %compare.3, bf16[4,512,128]{2,1,0:T(8,128)(2,1)} %get-tuple-element.167, s32[]{:T(128)} %get-tuple-element.154), kind=kOutput, calls=%fused_computation.6.clone.1 | convolution fusion | flops 537919488 | bytes 8520193 | tf_op jit(solution)/shard_map/while/body/eval_jaxpr/dot_general | solution.py:26
  87.7 12.9 %all_to_all.35 = bf16[8,256,128]{2,1,0:T(8,128)(2,1)} all-to-all(bf16[8,256,128]{2,1,0:T(8,128)(2,1)} %bitcast.64), channel_id=1, replica_groups=mesh['item'=32,'sub'=8] {'sub'}, dimensions={0} | all-to-all | bytes 1048576 | tf_op jit(solution)/shard_map/all_to_all | solution.py:54
  100.6 2.0 copy.13
  102.6 3.9 convolution_bitcast_fusion
  106.5 5.3 %copy.17 = f32[1024,1024]{1,0:T(8,128)} copy(f32[1024,1024]{0,1:T(8,128)} %convolution_bitcast_fusion) | data formatting | bytes 8388608
  114.7 127.1 %reduce-scatter.15.cloned.1.call-done = f32[32,1024]{1,0:T(8,128)} async-done(((f32[1024,1024]{1,0:T(8,128)}), f32[32,1024]{1,0:T(8,128)}) %reduce-scatter.15.cloned.1.call-update) | async-done | bytes 131088
  243.8 119.9 %reduce-scatter.13.cloned.1.call-done = f32[128,1]{1,0:T(8,128)} async-done(((f32[4096,1]{1,0:T(8,128)}), f32[128,1]{1,0:T(8,128)}) %reduce-scatter.13.cloned.1.call-update) | async-done | bytes 528
  364.6 120.5 %reduce-scatter.9.cloned.1.call-done = f32[1,128,128]{2,1,0:T(8,128)} async-done(((f32[1,4096,128]{2,1,0:T(8,128)}), f32[1,128,128]{2,1,0:T(8,128)}) %reduce-scatter.9.cloned.1.call-update) | async-done | bytes 65552 | tf_op jit(solution)/shard_map/reduce_scatter | solution.py:46
  486.8 36.5 %reduce-scatter.11.cloned.1.call-done = f32[32,128]{0,1:T(8,128)} async-done(((f32[32,1024]{0,1:T(8,128)}), f32[32,128]{0,1:T(8,128)}) %reduce-scatter.11.cloned.1.call-update) | async-done | bytes 16400 | tf_op jit(solution)/shard_map/reduce_scatter | solution.py:57
  (47 shorter events, 27.4 us)
Async XLA Ops:
  7.2 1.6 copy-start
  8.8 9.0 %copy-start.2 = (bf16[1,4096,128]{2,1,0:T(8,128)(2,1)S(1)}, bf16[1,4096,128]{2,1,0:T(8,128)(2,1)}, u32[]{:S(2)}) copy-start(bf16[1,4096,128]{2,1,0:T(8,128)(2,1)} %param.7) | copy-start | bytes 3145732
  11.5 14.0 %all-to-all-start = ((bf16[256,8,128]{2,0,1:T(8,128)(2,1)}), bf16[256,8,128]{2,0,1:T(8,128)(2,1)}, u32[]{:S(2)}, u32[]{:S(2)}) async-start(bf16[256,8,128]{2,0,1:T(8,128)(2,1)} %bitcast.61), calls=%async_computation | async-start | bytes 1048576 | tf_op jit(solution)/shard_map/all_to_all | solution.py:39
  17.7 224.2 %reduce-scatter.15.cloned.1.call-start = ((), (), s32[]{:S(2)}) async-start(), calls=%async_computation.9 | async-start | bytes 4325376
  33.5 5.0 copy-start.1
  48.6 5.7 %copy-start.1 = (bf16[512,4096]{1,0:T(8,128)(2,1)S(1)}, bf16[512,4096]{1,0:T(8,128)(2,1)}, u32[]{:S(2)}) copy-start(bf16[512,4096]{1,0:T(8,128)(2,1)} %get-tuple-element.144) | copy-start | bytes 12582916 | tf_op jit(solution)/shard_map/while
  64.3 5.7 %copy-start.1 = (bf16[512,4096]{1,0:T(8,128)(2,1)S(1)}, bf16[512,4096]{1,0:T(8,128)(2,1)}, u32[]{:S(2)}) copy-start(bf16[512,4096]{1,0:T(8,128)(2,1)} %get-tuple-element.144) | copy-start | bytes 12582916 | tf_op jit(solution)/shard_map/while
  80.0 5.7 %copy-start.1 = (bf16[512,4096]{1,0:T(8,128)(2,1)S(1)}, bf16[512,4096]{1,0:T(8,128)(2,1)}, u32[]{:S(2)}) copy-start(bf16[512,4096]{1,0:T(8,128)(2,1)} %get-tuple-element.144) | copy-start | bytes 12582916 | tf_op jit(solution)/shard_map/while
  111.9 251.8 %reduce-scatter.13.cloned.1.call-start = ((), (), s32[]{:S(2)}) async-start(), calls=%async_computation.8 | async-start | bytes 2162688
  114.0 371.2 %reduce-scatter.9.cloned.1.call-start = ((), (), s32[]{:S(2)}) async-start(), calls=%async_computation.6 | async-start | bytes 2162688 | tf_op jit(solution)/shard_map/reduce_scatter | solution.py:46
  114.7 408.5 %reduce-scatter.11.cloned.1.call-start = ((), (), s32[]{:S(2)}) async-start(), calls=%async_computation.7 | async-start | bytes 589824 | tf_op jit(solution)/shard_map/reduce_scatter | solution.py:57
Sparse Core Ops, SparseCore 0:
  112.0 129.8 reduce-scatter.14
  246.6 117.0 reduce-scatter.12
  367.9 117.2 reduce-scatter.8
  487.7 35.4 reduce-scatter.10
where the time goes:
time: 534 us; the launch traced here: 531 us
  waiting for transfers between devices  412 us (77%)
  matrix products  44.6 us (8%)
  other arithmetic  26.3 us (5%)
  local copies, waits for them, and re-layouts  15.4 us (3%)
  between operations  13.8 us (3%)
  blocking collectives  12.9 us (2%)
  starting transfers between devices  6.34 us (1%)
    unnamed x6, waiting for transfers between devices  248 us
    reduce_scatter x1, waiting for transfers between devices, body(): lax.psum_scatter(all_totals, 'item', scatter_dimension=1, tiled=True)  121 us
    reduce_scatter x1, waiting for transfers between devices, body(): lax.psum_scatter(item_cov, 'sub', scatter_dimension=1, tiled=True)  36.5 us
    dot_general x4, matrix products, step(): jnp.dot(weights.T, block, preferred_element_type=jnp.float32)  22.2 us
    reduce_sum x4, other arithmetic, step(): counts = counts + jnp.sum(weights.astype(jnp.float32), axis=0)  15.2 us
    all_to_all x1, blocking collectives, body(): lax.all_to_all(rebuilt, 'sub', split_axis=0, concat_axis=1, tiled=True)  12.9 us
    unnamed x9, local copies, waits for them, and re-layouts  12.4 us
  transfers between devices with their start and end apart: 5, of which 5 were waited for; matrix products, arithmetic and copies ran while one was open for 1% of the time, Pallas kernels for 0%

commit v1 on v0

v1 whole, which is shorter than its diff:
```python
import math

import jax
import jax.numpy as jnp
from jax import lax
from jax.experimental import pallas as pl
from jax.experimental.pallas import tpu as pltpu
from jax.sharding import PartitionSpec as P

BF = jnp.bfloat16
F32 = jnp.float32
MESH = pl.DeviceIdType.MESH
NT = (((1,), (1,)), ((), ()))

D, S, K, ROWS, SUBS, CHIPS = 1024, 128, 4096, 256, 8, 16
KC = 512
TC = 512
EXT = S + 16
SCALE = 3.0 / math.sqrt(S) * math.log2(math.e)


def kernel(
    samples_hbm, rotation_hbm, codebook_hbm,
    fresh_ref, cross_ref,
    samples, rotation, codes, codes_aug, codes_ext,
    sam_t, sam_sib,
    z_send, z_recv, zl, logits_a, logits_b, weights,
    reb_send, reb_recv, reb_sib,
    cov_own, cov_send, cov_recv, cov2_own, cov2_send, cov2_recv,
    tot_f, tot_b, tot_sib, tot_own, tot_send, tot_recv,
    load_sem, z_ss, z_rs, r_ss, r_rs, f_ss, f_rs, s_ss, s_rs,
    c_ss, c_rs, c2_ss, c2_rs, ts_ss, ts_rs, t_ss, t_rs,
):
    item, sub = lax.axis_index("item"), lax.axis_index("sub")
    core, chip = item % 2, item // 2
    sibling = item + 1 - 2 * core
    xl, y = sub // 4, sub % 4

    loads = [
        pltpu.make_async_copy(samples_hbm, samples, load_sem.at[0]),
        pltpu.make_async_copy(rotation_hbm, rotation, load_sem.at[1]),
        pltpu.make_async_copy(codebook_hbm.at[0], codes, load_sem.at[2]),
    ]
    for load in loads:
        load.start()

    barrier = pltpu.get_barrier_semaphore()

    def greet(i, s):
        pl.semaphore_signal(barrier, inc=1, device_id={"item": i, "sub": s}, device_id_type=MESH)

    def greet_sub(j, carry):
        greet(item, (sub + j) % SUBS)
        return carry

    def greet_chip(j, carry):
        greet((chip + j) % CHIPS * 2 + core, sub)
        return carry

    lax.fori_loop(1, SUBS, greet_sub, 0)
    lax.fori_loop(1, CHIPS, greet_chip, 0)
    greet(sibling, sub)

    def remote(src, dst, ss, rs, i, s):
        return pltpu.make_async_remote_copy(
            src_ref=src, dst_ref=dst, send_sem=ss, recv_sem=rs,
            device_id={"item": i, "sub": s}, device_id_type=MESH,
        )

    def z_copy(dest, src):
        return remote(z_send.at[dest], z_recv.at[src], z_ss.at[dest], z_rs.at[src], item, dest)

    def r_copy(dest, src):
        return remote(reb_send.at[dest], reb_recv.at[src], r_ss.at[dest], r_rs.at[src], item, dest)

    def f_copy(m):
        return remote(reb_recv.at[m], reb_sib.at[m], f_ss.at[m], f_rs.at[m], sibling, sub)

    def s_copy():
        return remote(sam_t.at[1 - core], sam_sib, s_ss, s_rs, sibling, sub)

    def c_copy(dest, src):
        return remote(cov_send.at[dest], cov_recv.at[src], c_ss.at[dest], c_rs.at[src], item, dest)

    def c2_copy(dest, src):
        return remote(
            cov2_send.at[dest], cov2_recv.at[src], c2_ss.at[dest], c2_rs.at[src], dest * 2 + core, sub
        )

    def ts_copy(g):
        return remote(tot_b.at[g, 1 - core], tot_sib.at[g], ts_ss.at[g], ts_rs.at[g], sibling, sub)

    def t_copy(dest, src):
        return remote(
            tot_send.at[dest], tot_recv.at[src], t_ss.at[dest], t_rs.at[src], dest * 2 + core, sub
        )

    def owner(t):
        return (xl + t // 4) % 2 * 4 + (y + t) % 4

    def origin(t):
        return (xl + t // 4) % 2 * 4 + (y + 8 - t) % 4

    loads[0].wait()
    loads[1].wait()
    pl.semaphore_wait(barrier, SUBS - 1 + CHIPS - 1 + 1)

    for step in range(4):
        pair = (sub // 2 + step) % 4
        rotated = jnp.dot(
            samples[...], rotation[:, pl.ds(pl.multiple_of(pair * 256, 256), 256)],
            preferred_element_type=F32,
        )
        rotated_t = rotated.T.astype(BF)
        for half in range(2):
            m = pair * 2 + half
            z_send[m] = rotated_t[half * S:(half + 1) * S]

            @pl.when(m != sub)
            def _():
                z_copy(m, sub).start()

    z_recv[sub] = z_send[sub]

    for piece in range(8):
        turned = samples[:, piece * 128:(piece + 1) * 128].astype(F32).T.astype(BF)
        for run in range(4):
            sam_t[run % 2, piece * 64 + run // 2 * 32:piece * 64 + run // 2 * 32 + 32] = turned[
                run * 32:(run + 1) * 32
            ]
    s_copy().start()

    loads[2].wait()
    lane = lax.broadcasted_iota(jnp.int32, (KC, S), 1)

    def prepare(j, carry):
        rows = pl.ds(pl.multiple_of(j * KC, KC), KC)
        code = codes[rows, :]
        code_f = code.astype(F32)
        bias = -0.5 * jnp.sum(code_f * code_f, axis=1, keepdims=True)
        high = bias.astype(BF).astype(F32)
        rest = bias - high
        mid = rest.astype(BF).astype(F32)
        low = rest - mid
        codes_aug[rows, :S] = code
        codes_aug[rows, S:] = jnp.where(
            lane == 0, high, jnp.where(lane == 1, mid, jnp.where(lane == 2, low, 0.0))
        ).astype(BF)
        codes_ext[:S, rows] = code_f.T.astype(BF)
        codes_ext[S:, rows] = jnp.ones((16, KC), BF)
        return carry

    lax.fori_loop(0, K // KC, prepare, 0)

    ones = jnp.ones((S, ROWS), BF)
    low_start = jnp.full((8, ROWS), -jnp.inf, F32)
    acc_start = jnp.zeros((EXT, ROWS), F32)
    logits = (logits_a, logits_b)
    row16 = lax.broadcasted_iota(jnp.int32, (16, ROWS), 0)

    def first(z_aug, j, out, top):
        rows = pl.ds(j * KC, KC)
        value = jnp.dot(codes_aug[rows, :], z_aug, preferred_element_type=F32)
        out[rows, :] = value
        return jnp.maximum(top, jnp.max(value.reshape(KC // 8, 8, ROWS), axis=0))

    def second(cols, j, src, top, acc):
        rows = pl.ds(j * KC, KC)
        w = jnp.exp2(src[rows, :] * SCALE - top).astype(BF)
        weights[rows, cols] = w
        return acc + jnp.dot(codes_ext[:, rows], w, preferred_element_type=F32)

    def finish(t, cols, acc):
        who = owner(t)
        inverse = 1.0 / acc[S:S + 1]
        rebuilt = (acc[:S] * inverse).astype(BF)
        zl[:S, cols] = (z_recv[who].astype(F32) * inverse).astype(BF)
        high = inverse.astype(BF).astype(F32)
        zl[S:, cols] = jnp.where(row16 == 0, high, jnp.where(row16 == 1, inverse - high, 0.0)).astype(BF)
        return who, rebuilt

    def forward(t):
        m = origin(t)

        @pl.when(t != 0)
        def _():
            r_copy(sub, m).wait_recv()

        f_copy(m).start()

    def cross(t):
        m = origin(t)
        f_copy(m).wait_recv()
        part = lax.dot_general(sam_t[core], reb_recv[m], NT, preferred_element_type=F32)
        part = part + lax.dot_general(sam_sib[...], reb_sib[m], NT, preferred_element_type=F32)

        @pl.when(t == 0)
        def _():
            cov_own[...] = part

        @pl.when(t != 0)
        def _():
            cov_send[m] = part.astype(BF)
            c_copy(m, sub).start()

    z0 = jnp.concatenate([z_recv[sub], ones], 0)
    top = low_start
    for j in range(K // KC):
        top = first(z0, j, logits_a, top)
    s_copy().wait_recv()

    def two_steps(tt, top):
        for half in range(2):
            t = tt * 2 + half
            cols = pl.ds(pl.multiple_of(t * ROWS, ROWS), ROWS)

            @pl.when(t < SUBS - 1)
            def _():
                z_copy(sub, owner(t + 1)).wait_recv()

            z_next = jnp.concatenate([z_recv[owner(t + 1)], ones], 0)
            level = jnp.max(top, axis=0, keepdims=True) * SCALE
            acc, top = acc_start, low_start
            for j in range(K // KC):
                acc = second(cols, j, logits[half], level, acc)
                top = first(z_next, j, logits[1 - half], top)
            who, rebuilt = finish(t, cols, acc)

            @pl.when(t == 0)
            def _():
                reb_recv[sub] = rebuilt

            @pl.when(t != 0)
            def _():
                reb_send[who] = rebuilt
                r_copy(who, sub).start()

            @pl.when(tt >= 1)
            def _():
                forward(t - 2)

            @pl.when(tt >= 2)
            def _():
                cross(t - 4)

        return top

    lax.fori_loop(0, SUBS // 2, two_steps, top)

    def sums(j):
        g = (chip // 2 + 1 + j) % 8
        value = lax.dot_general(
            weights[pl.ds(pl.multiple_of(g * TC, TC), TC), :], zl[...], NT, preferred_element_type=F32
        )
        for h in range(2):
            for p in range(2):
                block = value[(h * 2 + p) * 128:(h * 2 + p + 1) * 128]
                counts = block[:, S:].T
                tot_f[g, p, h, :S] = block[:, :S]
                tot_f[g, p, h, S:] = counts
                tot_b[g, p, h, :S] = block[:, :S].astype(BF)
                tot_b[g, p, h, S:] = counts.astype(BF)
        ts_copy(g).start()

    def share(j):
        g = (chip // 2 + 1 + j) % 8
        ts_copy(g).wait_recv()
        for h in range(2):
            q = g * 2 + h
            both = tot_f[g, core, h] + tot_sib[g, h].astype(F32)

            @pl.when(q == chip)
            def _():
                tot_own[...] = both

            @pl.when(q != chip)
            def _():
                tot_send[q] = both.astype(BF)
                t_copy(q, chip).start()

    def sums_step(j, carry):
        sums(j)

        @pl.when(j >= 2)
        def _():
            share(j - 2)

        @pl.when(j < 2)
        def _():
            forward(6 + j)

        @pl.when(j < 4)
        def _():
            cross(4 + j)

        return carry

    lax.fori_loop(0, 8, sums_step, 0)
    share(6)
    share(7)

    def gather_cov(j, carry):
        src = (sub + j) % SUBS
        c_copy(sub, src).wait_recv()
        cov_own[...] = cov_own[...] + cov_recv[src].astype(F32)
        return carry

    lax.fori_loop(1, SUBS, gather_cov, 0)

    def spread_cov(j, carry):
        q = (chip + j) % CHIPS
        cov2_send[q] = cov_own[pl.ds(pl.multiple_of(q * 32, 32), 32), :].astype(BF)
        c2_copy(q, chip).start()
        return carry

    lax.fori_loop(1, CHIPS, spread_cov, 0)

    def gather_tot(j, acc):
        src = (chip + j) % CHIPS
        t_copy(chip, src).wait_recv()
        return acc + tot_recv[src].astype(F32)

    total = lax.fori_loop(1, CHIPS, gather_tot, tot_own[...])
    count = jnp.broadcast_to(total[S:S + 1] + total[S + 1:S + 2] + 1.0, (128, 128)).T
    mine = codes[pl.ds(pl.multiple_of(item * 128, 128), 128), :].astype(F32)
    fresh_ref[0] = (total[:S] + mine) / count

    def gather_cov2(j, acc):
        src = (chip + j) % CHIPS
        c2_copy(chip, src).wait_recv()
        return acc + cov2_recv[src].astype(F32)

    cross_ref[...] = lax.fori_loop(
        1, CHIPS, gather_cov2, cov_own[pl.ds(pl.multiple_of(chip * 32, 32), 32), :]
    )

    def sent_sub(j, carry):
        other = (sub + j) % SUBS
        z_copy(other, sub).wait_send()
        r_copy(other, sub).wait_send()
        c_copy(other, sub).wait_send()
        return carry

    def sent_all(j, carry):
        f_copy(j).wait_send()
        ts_copy(j).wait_send()
        return carry

    def sent_chip(j, carry):
        other = (chip + j) % CHIPS
        t_copy(other, chip).wait_send()
        c2_copy(other, chip).wait_send()
        return carry

    lax.fori_loop(1, SUBS, sent_sub, 0)
    lax.fori_loop(0, SUBS, sent_all, 0)
    lax.fori_loop(1, CHIPS, sent_chip, 0)
    s_copy().wait_send()


def body(samples, rotation, codebook):
    dma = pltpu.SemaphoreType.DMA
    return pl.pallas_call(
        kernel,
        out_shape=(
            jax.ShapeDtypeStruct((1, 128, S), F32),
            jax.ShapeDtypeStruct((32, 128), F32),
        ),
        in_specs=[pl.BlockSpec(memory_space=pl.ANY)] * 3,
        out_specs=[pl.BlockSpec(memory_space=pltpu.VMEM)] * 2,
        scratch_shapes=[
            pltpu.VMEM((ROWS, D), BF),
            pltpu.VMEM((D, D), BF),
            pltpu.VMEM((K, S), BF),
            pltpu.VMEM((K, 2 * S), BF),
            pltpu.VMEM((EXT, K), BF),
            pltpu.VMEM((2, D // 2, ROWS), BF),
            pltpu.VMEM((D // 2, ROWS), BF),
            pltpu.VMEM((SUBS, S, ROWS), BF),
            pltpu.VMEM((SUBS, S, ROWS), BF),
            pltpu.VMEM((EXT, SUBS * ROWS), BF),
            pltpu.VMEM((K, ROWS), F32),
            pltpu.VMEM((K, ROWS), F32),
            pltpu.VMEM((K, SUBS * ROWS), BF),
            pltpu.VMEM((SUBS, S, ROWS), BF),
            pltpu.VMEM((SUBS, S, ROWS), BF),
            pltpu.VMEM((SUBS, S, ROWS), BF),
            pltpu.VMEM((D // 2, S), F32),
            pltpu.VMEM((SUBS, D // 2, S), BF),
            pltpu.VMEM((SUBS, D // 2, S), BF),
            pltpu.VMEM((32, S), F32),
            pltpu.VMEM((CHIPS, 32, S), BF),
            pltpu.VMEM((CHIPS, 32, S), BF),
            pltpu.VMEM((8, 2, 2, EXT, S), F32),
            pltpu.VMEM((8, 2, 2, EXT, S), BF),
            pltpu.VMEM((8, 2, EXT, S), BF),
            pltpu.VMEM((EXT, S), F32),
            pltpu.VMEM((CHIPS, EXT, S), BF),
            pltpu.VMEM((CHIPS, EXT, S), BF),
            dma((3,)),
            dma((SUBS,)), dma((SUBS,)),
            dma((SUBS,)), dma((SUBS,)),
            dma((SUBS,)), dma((SUBS,)),
            dma, dma,
            dma((SUBS,)), dma((SUBS,)),
            dma((CHIPS,)), dma((CHIPS,)),
            dma((8,)), dma((8,)),
            dma((CHIPS,)), dma((CHIPS,)),
        ],
        compiler_params=pltpu.CompilerParams(
            collective_id=0, has_side_effects=True, vmem_limit_bytes=58 * 2**20
        ),
        cost_estimate=pl.CostEstimate(
            flops=8 * 10**9, bytes_accessed=4 * 2**20, transcendentals=K * SUBS * ROWS
        ),
        name="quantize",
    )(samples, rotation, codebook)


def solution(mesh):
    return jax.shard_map(
        body,
        mesh=mesh,
        in_specs=(P(("item", "sub"), None), P(), P("sub", None, None)),
        out_specs=(P("sub", "item", None), P("item", "sub")),
        check_vma=False,
    )
```

time: 534 us -> 64.8 us (0.12)
  waiting for transfers between devices: 412 us -> 0 us
  Pallas kernels: 0 us -> 61.1 us
  matrix products: 44.6 us -> 0 us
  other arithmetic: 26.3 us -> 0 us
  between operations: 13.8 us -> 0.64 us
  blocking collectives: 12.9 us -> 0 us
  local copies, waits for them, and re-layouts: 15.4 us -> 2.8 us
  starting transfers between devices: 6.34 us -> 0 us
    unnamed x6 -> x0, waiting for transfers between devices: 248 us -> none
    reduce_scatter x2 -> x0, waiting for transfers between devices: 157 us -> none  [the longest x1 121 us: body(): lax.psum_scatter(all_totals, 'item', scatter_dimension=1, tiled=True)]
    pallas_call x0 -> x1, Pallas kernels: none -> 61.1 us  [body(): pl.pallas_call(kernel, out_shape=(jax.ShapeDtypeStruct((1, 128, S), F32),...]
    dot_general x14 -> x0, matrix products: 44.6 us -> none  [the longest x4 22.2 us: step(): jnp.dot(weights.T, block, preferred_element_type=jnp.float32)]
    reduce_sum x9 -> x0, other arithmetic: 23.8 us -> none  [the longest x4 15.2 us: step(): counts = counts + jnp.sum(weights.astype(jnp.float32), axis=0)]
    all_to_all x1 -> x0, blocking collectives: 12.9 us -> none  [body(): lax.all_to_all(rebuilt, 'sub', split_axis=0, concat_axis=1, tiled=True)]
    unnamed x9 -> x2, local copies, waits for them, and re-layouts: 12.4 us -> 2.8 us
    all_to_all x1 -> x0, waiting for transfers between devices: 7.11 us -> none  [body(): lax.all_to_all(rotated, 'sub', split_axis=1, concat_axis=0, tiled=True)]
  transfers between devices with their start and end apart: 5 -> 0, of which waited for: 5 -> 0; matrix products, arithmetic and copies ran while one was open for 1% -> 0% of each run, Pallas kernels for 0% -> 0%
where the time goes in v1:
time: 64.8 us; the launch traced here: 64.6 us
  Pallas kernels  61.1 us (94%)
  local copies, waits for them, and re-layouts  2.8 us (4%)
    pallas_call x1, Pallas kernels, body(): pl.pallas_call(kernel, out_shape=(jax.ShapeDtypeStruct((1, 128, S), F32),...  61.1 us
    unnamed x2, local copies, waits for them, and re-layouts  2.8 us

profile of v1, /device:TPU:8, one launch (start us, length us, event | category | flops | bytes accessed | tf_op | source)
XLA Modules:
  0.0 64.6 jit_solution(12034710131283067992)
XLA Ops:
  0.6 61.1 %quantize.1 = (f32[1,128,128]{2,1,0:T(8,128)}, f32[32,128]{1,0:T(8,128)}) custom-call(bf16[256,1024]{1,0:T(8,128)(2,1)} %samples_hbm.1, bf16[1024,1024]{1,0:T(8,128)(2,1)} %rotation_hbm.1, bf16[1,4096,128]{2,1,0:T(8,128)(2,1)} %codebook_hbm.1), custom_call_target="tpu_custom_call" | custom-call | flops 8000000000 | bytes 4194304 | tf_op jit(solution)/shard_map/quantize/pallas_call | solution.py:363
  61.8 1.5 %copy.7 = f32[1,128,128]{2,1,0:T(8,128)} copy(f32[1,128,128]{2,1,0:T(8,128)} %get-tuple-element.4) | data formatting | bytes 131072
  63.3 1.3 %copy.8 = f32[32,128]{1,0:T(8,128)} copy(f32[32,128]{1,0:T(8,128)} %get-tuple-element.5) | data formatting | bytes 32768

commit v2 on v1

--- a/solution.py
+++ b/solution.py
@@ -12,9 +12,10 @@
 MESH = pl.DeviceIdType.MESH
 NT = (((1,), (1,)), ((), ()))
 
-D, S, K, ROWS, SUBS, CHIPS = 1024, 128, 4096, 256, 8, 16
+D, S, K, ROWS, SUBS = 1024, 128, 4096, 256, 8
 KC = 512
 TC = 512
+LAG_F, LAG_C = 3, 5
 EXT = S + 16
 SCALE = 3.0 / math.sqrt(S) * math.log2(math.e)
 
@@ -26,15 +27,19 @@
     sam_t, sam_sib,
     z_send, z_recv, zl, logits_a, logits_b, weights,
     reb_send, reb_recv, reb_sib,
-    cov_own, cov_send, cov_recv, cov2_own, cov2_send, cov2_recv,
-    tot_f, tot_b, tot_sib, tot_own, tot_send, tot_recv,
+    cov_send, a_own, a_recv, b_own, b_recv, a2_own, a2_send, a2_recv, b2_own, b2_send, b2_recv,
+    fin, c3_send, c3_recv,
+    tot_f, tot_b, tot_sib, tot_own, tot_x, x_recv, tot_send, tot_recv,
     load_sem, z_ss, z_rs, r_ss, r_rs, f_ss, f_rs, s_ss, s_rs,
-    c_ss, c_rs, c2_ss, c2_rs, ts_ss, ts_rs, t_ss, t_rs,
+    a_ss, a_rs, b_ss, b_rs, a2_ss, a2_rs, b2_ss, b2_rs, c3_ss, c3_rs,
+    ts_ss, ts_rs, tx_ss, tx_rs, t_ss, t_rs,
 ):
     item, sub = lax.axis_index("item"), lax.axis_index("sub")
     core, chip = item % 2, item // 2
     sibling = item + 1 - 2 * core
     xl, y = sub // 4, sub % 4
+    xh, z = chip // 8, chip % 8
+    x = xh * 2 + xl
 
     loads = [
         pltpu.make_async_copy(samples_hbm, samples, load_sem.at[0]),
@@ -53,12 +58,15 @@
         greet(item, (sub + j) % SUBS)
         return carry
 
-    def greet_chip(j, carry):
-        greet((chip + j) % CHIPS * 2 + core, sub)
+    def greet_z(j, carry):
+        greet((xh * 8 + (z + j) % 8) * 2 + core, sub)
         return carry
 
     lax.fori_loop(1, SUBS, greet_sub, 0)
-    lax.fori_loop(1, CHIPS, greet_chip, 0)
+    lax.fori_loop(1, 8, greet_z, 0)
+    across = ((1 - xh) * 8 + z) * 2 + core
+    greet(across, sub)
+    greet(across, (1 - xl) * 4 + y)
     greet(sibling, sub)
 
     def remote(src, dst, ss, rs, i, s):
@@ -79,31 +87,57 @@
     def s_copy():
         return remote(sam_t.at[1 - core], sam_sib, s_ss, s_rs, sibling, sub)
 
-    def c_copy(dest, src):
-        return remote(cov_send.at[dest], cov_recv.at[src], c_ss.at[dest], c_rs.at[src], item, dest)
-
-    def c2_copy(dest, src):
+    def along_x(dest):
+        return (dest // 2 * 8 + z) * 2 + core, dest % 2 * 4 + y
+
+    def a_copy(dest, ym, src):
         return remote(
-            cov2_send.at[dest], cov2_recv.at[src], c2_ss.at[dest], c2_rs.at[src], dest * 2 + core, sub
+            cov_send.at[dest % 2 * 4 + ym, 0, dest // 2], a_recv.at[src, ym],
+            a_ss.at[dest, ym], a_rs.at[src, ym], *along_x(dest),
+        )
+
+    def b_copy(dest, xm, src):
+        return remote(
+            cov_send.at[xm * 4 + dest, 1], b_recv.at[src, xm],
+            b_ss.at[dest, xm], b_rs.at[src, xm], item, xl * 4 + dest,
+        )
+
+    def a2_copy(dest, src):
+        return remote(
+            a2_send.at[dest], a2_recv.at[src], a2_ss.at[dest], a2_rs.at[src], item, xl * 4 + dest
+        )
+
+    def b2_copy(dest, src):
+        return remote(
+            b2_send.at[dest], b2_recv.at[src], b2_ss.at[dest], b2_rs.at[src], *along_x(dest)
+        )
+
+    def c3_copy(dest, src):
+        return remote(
+            c3_send.at[dest], c3_recv.at[src], c3_ss.at[dest], c3_rs.at[src],
+            (xh * 8 + dest) * 2 + core, sub,
         )
 
     def ts_copy(g):
         return remote(tot_b.at[g, 1 - core], tot_sib.at[g], ts_ss.at[g], ts_rs.at[g], sibling, sub)
 
+    def tx_copy(zz):
+        return remote(tot_x.at[zz], x_recv.at[zz], tx_ss.at[zz], tx_rs.at[zz], across, sub)
+
     def t_copy(dest, src):
         return remote(
-            tot_send.at[dest], tot_recv.at[src], t_ss.at[dest], t_rs.at[src], dest * 2 + core, sub
+            tot_send.at[dest], tot_recv.at[src], t_ss.at[dest], t_rs.at[src],
+            (xh * 8 + dest) * 2 + core, sub,
         )
 
     def owner(t):
-        return (xl + t // 4) % 2 * 4 + (y + t) % 4
+        return (xl + t) % 2 * 4 + (y + t // 2) % 4
 
     def origin(t):
-        return (xl + t // 4) % 2 * 4 + (y + 8 - t) % 4
+        return (xl + t) % 2 * 4 + (y + 8 - t // 2) % 4
 
     loads[0].wait()
     loads[1].wait()
-    pl.semaphore_wait(barrier, SUBS - 1 + CHIPS - 1 + 1)
 
     for step in range(4):
         pair = (sub // 2 + step) % 4
@@ -116,10 +150,9 @@
             m = pair * 2 + half
             z_send[m] = rotated_t[half * S:(half + 1) * S]
 
-            @pl.when(m != sub)
-            def _():
-                z_copy(m, sub).start()
-
+    pl.semaphore_wait(barrier, 7 + 7 + 2 + 1)
+    for t in range(1, 4):
+        z_copy(origin(t), sub).start()
     z_recv[sub] = z_send[sub]
 
     for piece in range(8):
@@ -129,6 +162,8 @@
                 run * 32:(run + 1) * 32
             ]
     s_copy().start()
+    for t in range(4, 6):
+        z_copy(origin(t), sub).start()
 
     loads[2].wait()
     lane = lax.broadcasted_iota(jnp.int32, (KC, S), 1)
@@ -150,7 +185,10 @@
         codes_ext[S:, rows] = jnp.ones((16, KC), BF)
         return carry
 
-    lax.fori_loop(0, K // KC, prepare, 0)
+    lax.fori_loop(0, K // KC // 2, prepare, 0)
+    for t in range(6, SUBS):
+        z_copy(origin(t), sub).start()
+    lax.fori_loop(K // KC // 2, K // KC, prepare, 0)
 
     ones = jnp.ones((S, ROWS), BF)
     low_start = jnp.full((8, ROWS), -jnp.inf, F32)
@@ -194,14 +232,61 @@
         part = lax.dot_general(sam_t[core], reb_recv[m], NT, preferred_element_type=F32)
         part = part + lax.dot_general(sam_sib[...], reb_sib[m], NT, preferred_element_type=F32)
 
-        @pl.when(t == 0)
-        def _():
-            cov_own[...] = part
-
-        @pl.when(t != 0)
-        def _():
-            cov_send[m] = part.astype(BF)
-            c_copy(m, sub).start()
+        xm, ym = m // 4, m % 4
+        for xd in range(2):
+            dest = xd * 2 + xm
+            cov_send[m, 0, xd] = part[xd * 256:xd * 256 + 128].astype(BF)
+            cov_send[m, 1, xd] = part[xd * 256 + 128:xd * 256 + 256].astype(BF)
+
+            @pl.when(dest == x)
+            def _():
+                a_own[ym] = part[xd * 256:xd * 256 + 128]
+
+            @pl.when(dest != x)
+            def _():
+                a_copy(dest, ym, x).start()
+
+        @pl.when(ym == y)
+        def _():
+            for xd in range(2):
+                b_own[xm * 2 + xd] = part[xd * 256 + 128:xd * 256 + 256]
+
+        @pl.when(ym != y)
+        def _():
+            b_copy(ym, xm, y).start()
+
+    def gather_a(dy):
+        ym = (y + 4 - dy) % 4
+        acc = a_own[ym]
+        for k in range(1, 4):
+            src = (x + k) % 4
+            a_copy(x, ym, src).wait_recv()
+            acc = acc + a_recv[src, ym].astype(F32)
+        return ym, acc
+
+    def gather_b(k):
+        dest = (x + k) % 4
+        xm, xd = dest % 2, dest // 2
+        acc = b_own[xm * 2 + xd]
+        for j in range(1, 4):
+            acc = acc + b_recv[(y + j) % 4, xm, xd].astype(F32)
+        return dest, acc
+
+    def spread_a(dy):
+        ym, acc = gather_a(dy)
+        a2_send[ym] = acc.astype(BF)
+        a2_copy(ym, y).start()
+
+    def spread_b():
+        for j in range(1, 4):
+            for xm in range(2):
+                b_copy(y, xm, (y + j) % 4).wait_recv()
+        for k in range(1, 4):
+            dest, acc = gather_b(k)
+            b2_send[dest] = acc.astype(BF)
+            b2_copy(dest, x).start()
+        b2_own[...] = gather_b(0)[1]
+        a2_own[...] = gather_a(0)[1]
 
     z0 = jnp.concatenate([z_recv[sub], ones], 0)
     top = low_start
@@ -235,20 +320,23 @@
                 reb_send[who] = rebuilt
                 r_copy(who, sub).start()
 
-            @pl.when(tt >= 1)
-            def _():
-                forward(t - 2)
-
-            @pl.when(tt >= 2)
-            def _():
-                cross(t - 4)
+            @pl.when(t >= LAG_F)
+            def _():
+                forward(t - LAG_F)
+
+            @pl.when(t >= LAG_C)
+            def _():
+                cross(t - LAG_C)
 
         return top
 
     lax.fori_loop(0, SUBS // 2, two_steps, top)
 
+    def group(j):
+        return (xh + 1 + j // 4) % 2 * 4 + (z // 2 + 1 + j) % 4
+
     def sums(j):
-        g = (chip // 2 + 1 + j) % 8
+        g = group(j)
         value = lax.dot_general(
             weights[pl.ds(pl.multiple_of(g * TC, TC), TC), :], zl[...], NT, preferred_element_type=F32
         )
@@ -262,99 +350,131 @@
                 tot_b[g, p, h, S:] = counts.astype(BF)
         ts_copy(g).start()
 
-    def share(j):
-        g = (chip // 2 + 1 + j) % 8
+    def pair_sum(j):
+        g = group(j)
         ts_copy(g).wait_recv()
+        return g, [tot_f[g, core, h] + tot_sib[g, h].astype(F32) for h in range(2)]
+
+    def share_x(j):
+        g, both = pair_sum(j)
         for h in range(2):
-            q = g * 2 + h
-            both = tot_f[g, core, h] + tot_sib[g, h].astype(F32)
-
-            @pl.when(q == chip)
-            def _():
-                tot_own[...] = both
-
-            @pl.when(q != chip)
-            def _():
-                tot_send[q] = both.astype(BF)
-                t_copy(q, chip).start()
+            zz = g % 4 * 2 + h
+            tot_x[zz] = both[h].astype(BF)
+            tx_copy(zz).start()
+
+    def share_z(j):
+        g, both = pair_sum(j)
+        for h in range(2):
+            zz = g % 4 * 2 + h
+            tx_copy(zz).wait_recv()
+            four = both[h] + x_recv[zz].astype(F32)
+
+            @pl.when(zz == z)
+            def _():
+                tot_own[...] = four
+
+            @pl.when(zz != z)
+            def _():
+                tot_send[zz] = four.astype(BF)
+                t_copy(zz, z).start()
 
     def sums_step(j, carry):
         sums(j)
 
-        @pl.when(j >= 2)
-        def _():
-            share(j - 2)
-
-        @pl.when(j < 2)
-        def _():
-            forward(6 + j)
-
-        @pl.when(j < 4)
-        def _():
-            cross(4 + j)
+        @pl.when(j < LAG_F)
+        def _():
+            forward(SUBS - LAG_F + j)
+
+        @pl.when(j < LAG_C)
+        def _():
+            cross(SUBS - LAG_C + j)
+
+        @pl.when((j >= 2) & (j < 6))
+        def _():
+            share_x(j - 2)
+
+        @pl.when(j >= 6)
+        def _():
+            share_z(j - 2)
+
+        @pl.when((j % 2 == 0) & (j >= 2))
+        def _():
+            spread_a(j // 2)
 
         return carry
 
     lax.fori_loop(0, 8, sums_step, 0)
-    share(6)
-    share(7)
-
-    def gather_cov(j, carry):
-        src = (sub + j) % SUBS
-        c_copy(sub, src).wait_recv()
-        cov_own[...] = cov_own[...] + cov_recv[src].astype(F32)
-        return carry
-
-    lax.fori_loop(1, SUBS, gather_cov, 0)
-
-    def spread_cov(j, carry):
-        q = (chip + j) % CHIPS
-        cov2_send[q] = cov_own[pl.ds(pl.multiple_of(q * 32, 32), 32), :].astype(BF)
-        c2_copy(q, chip).start()
-        return carry
-
-    lax.fori_loop(1, CHIPS, spread_cov, 0)
+    spread_b()
+    share_z(6)
+    share_z(7)
+
+    acc = a2_own[...]
+    for k in range(1, 4):
+        a2_copy(y, (y + k) % 4).wait_recv()
+        acc = acc + a2_recv[(y + k) % 4].astype(F32)
+    fin[:128] = acc
+    acc = b2_own[...]
+    for k in range(1, 4):
+        b2_copy(x, (x + k) % 4).wait_recv()
+        acc = acc + b2_recv[(x + k) % 4].astype(F32)
+    fin[128:] = acc
+
+    def spread_c(j, carry):
+        zz = (z + j) % 8
+        c3_send[zz] = fin[pl.ds(pl.multiple_of(zz * 32, 32), 32), :].astype(BF)
+        c3_copy(zz, z).start()
+        return carry
+
+    lax.fori_loop(1, 8, spread_c, 0)
 
     def gather_tot(j, acc):
-        src = (chip + j) % CHIPS
-        t_copy(chip, src).wait_recv()
+        src = (z + j) % 8
+        t_copy(z, src).wait_recv()
         return acc + tot_recv[src].astype(F32)
 
-    total = lax.fori_loop(1, CHIPS, gather_tot, tot_own[...])
+    total = lax.fori_loop(1, 8, gather_tot, tot_own[...])
     count = jnp.broadcast_to(total[S:S + 1] + total[S + 1:S + 2] + 1.0, (128, 128)).T
     mine = codes[pl.ds(pl.multiple_of(item * 128, 128), 128), :].astype(F32)
     fresh_ref[0] = (total[:S] + mine) / count
 
-    def gather_cov2(j, acc):
-        src = (chip + j) % CHIPS
-        c2_copy(chip, src).wait_recv()
-        return acc + cov2_recv[src].astype(F32)
-
-    cross_ref[...] = lax.fori_loop(
-        1, CHIPS, gather_cov2, cov_own[pl.ds(pl.multiple_of(chip * 32, 32), 32), :]
-    )
+    def gather_c(j, acc):
+        src = (z + j) % 8
+        c3_copy(z, src).wait_recv()
+        return acc + c3_recv[src].astype(F32)
+
+    cross_ref[...] = lax.fori_loop(1, 8, gather_c, fin[pl.ds(pl.multiple_of(z * 32, 32), 32), :])
 
     def sent_sub(j, carry):
         other = (sub + j) % SUBS
         z_copy(other, sub).wait_send()
         r_copy(other, sub).wait_send()
-        c_copy(other, sub).wait_send()
         return carry
 
     def sent_all(j, carry):
         f_copy(j).wait_send()
         ts_copy(j).wait_send()
-        return carry
-
-    def sent_chip(j, carry):
-        other = (chip + j) % CHIPS
-        t_copy(other, chip).wait_send()
-        c2_copy(other, chip).wait_send()
+        tx_copy(j).wait_send()
+        return carry
+
+    def sent_z(j, carry):
+        other = (z + j) % 8
+        t_copy(other, z).wait_send()
+        c3_copy(other, z).wait_send()
+        return carry
+
+    def sent_ring(j, carry):
+        for ym in range(4):
+            a_copy((x + j) % 4, ym, x).wait_send()
+        for xm in range(2):
+            b_copy((y + j) % 4, xm, y).wait_send()
+        a2_copy((y + j) % 4, y).wait_send()
+        b2_copy((x + j) % 4, x).wait_send()
         return carry
 
     lax.fori_loop(1, SUBS, sent_sub, 0)
     lax.fori_loop(0, SUBS, sent_all, 0)
-    lax.fori_loop(1, CHIPS, sent_chip, 0)
+    lax.fori_loop(1, 8, sent_z, 0)
+    lax.fori_loop(1, 4, sent_ring, 0)
     s_copy().wait_send()
 
 
@@ -385,27 +505,41 @@
             pltpu.VMEM((SUBS, S, ROWS), BF),
             pltpu.VMEM((SUBS, S, ROWS), BF),
             pltpu.VMEM((SUBS, S, ROWS), BF),
-            pltpu.VMEM((D // 2, S), F32),
-            pltpu.VMEM((SUBS, D // 2, S), BF),
-            pltpu.VMEM((SUBS, D // 2, S), BF),
-            pltpu.VMEM((32, S), F32),
-            pltpu.VMEM((CHIPS, 32, S), BF),
-            pltpu.VMEM((CHIPS, 32, S), BF),
+            pltpu.VMEM((SUBS, 2, 2, 128, S), BF),
+            pltpu.VMEM((4, 128, S), F32),
+            pltpu.VMEM((4, 4, 128, S), BF),
+            pltpu.VMEM((4, 128, S), F32),
+            pltpu.VMEM((4, 2, 2, 128, S), BF),
+            pltpu.VMEM((128, S), F32),
+            pltpu.VMEM((4, 128, S), BF),
+            pltpu.VMEM((4, 128, S), BF),
+            pltpu.VMEM((128, S), F32),
+            pltpu.VMEM((4, 128, S), BF),
+            pltpu.VMEM((4, 128, S), BF),
+            pltpu.VMEM((256, S), F32),
+            pltpu.VMEM((8, 32, S), BF),
+            pltpu.VMEM((8, 32, S), BF),
             pltpu.VMEM((8, 2, 2, EXT, S), F32),
             pltpu.VMEM((8, 2, 2, EXT, S), BF),
             pltpu.VMEM((8, 2, EXT, S), BF),
             pltpu.VMEM((EXT, S), F32),
-            pltpu.VMEM((CHIPS, EXT, S), BF),
-            pltpu.VMEM((CHIPS, EXT, S), BF),
+            pltpu.VMEM((8, EXT, S), BF),
+            pltpu.VMEM((8, EXT, S), BF),
+            pltpu.VMEM((8, EXT, S), BF),
+            pltpu.VMEM((8, EXT, S), BF),
             dma((3,)),
             dma((SUBS,)), dma((SUBS,)),
             dma((SUBS,)), dma((SUBS,)),
             dma((SUBS,)), dma((SUBS,)),
             dma, dma,
-            dma((SUBS,)), dma((SUBS,)),
-            dma((CHIPS,)), dma((CHIPS,)),
+            dma((4, 4)), dma((4, 4)),
+            dma((4, 2)), dma((4, 2)),
+            dma((4,)), dma((4,)),
+            dma((4,)), dma((4,)),
             dma((8,)), dma((8,)),
-            dma((CHIPS,)), dma((CHIPS,)),
+            dma((8,)), dma((8,)),
+            dma((8,)), dma((8,)),
+            dma((8,)), dma((8,)),
         ],
         compiler_params=pltpu.CompilerParams(
             collective_id=0, has_side_effects=True, vmem_limit_bytes=58 * 2**20

time: 64.8 us -> 56.5 us (0.87)
  the two profiles are of different devices: /device:TPU:8 before, /device:TPU:30 now
where the time goes in v2:
time: 56.5 us; the launch traced here: 56.3 us
  Pallas kernels  52.8 us (93%)
  local copies, waits for them, and re-layouts  2.8 us (5%)
  between operations  0.64 us (1%)
    pallas_call x1, Pallas kernels, body(): pl.pallas_call(kernel, out_shape=(jax.ShapeDtypeStruct((1, 128, S), F32),...  52.8 us
    unnamed x2, local copies, waits for them, and re-layouts  2.8 us

profile of v2, /device:TPU:30, one launch (start us, length us, event | category | flops | bytes accessed | tf_op | source)
XLA Modules:
  0.0 56.3 jit_solution(4705221085512878055)
XLA Ops:
  0.6 52.8 %quantize.1 = (f32[1,128,128]{2,1,0:T(8,128)}, f32[32,128]{1,0:T(8,128)}) custom-call(bf16[256,1024]{1,0:T(8,128)(2,1)} %samples_hbm.1, bf16[1024,1024]{1,0:T(8,128)(2,1)} %rotation_hbm.1, bf16[1,4096,128]{2,1,0:T(8,128)(2,1)} %codebook_hbm.1), custom_call_target="tpu_custom_call" | custom-call | flops 8000000000 | bytes 4194304 | tf_op jit(solution)/shard_map/quantize/pallas_call | solution.py:483
  53.5 1.5 %copy.7 = f32[1,128,128]{2,1,0:T(8,128)} copy(f32[1,128,128]{2,1,0:T(8,128)} %get-tuple-element.4) | data formatting | bytes 131072
  54.9 1.3 %copy.8 = f32[32,128]{1,0:T(8,128)} copy(f32[32,128]{1,0:T(8,128)} %get-tuple-element.5) | data formatting | bytes 32768

commit v3 on v2

--- a/solution.py
+++ b/solution.py
@@ -15,7 +15,11 @@
 D, S, K, ROWS, SUBS = 1024, 128, 4096, 256, 8
 KC = 512
 TC = 512
-LAG_F, LAG_C = 3, 5
+LAG_F, LAG_C = 4, 6
+FORWARDS = {0: (4,), 1: (5,), 2: (6, 7)}
+CROSSES = {0: (2,), 1: (3,), 2: (4,), 3: (5,), 4: (6, 7)}
+SPREADS = {5: (1,), 6: (2,), 7: (3,)}
+SPREAD_B = 8
 EXT = S + 16
 SCALE = 3.0 / math.sqrt(S) * math.log2(math.e)
 
@@ -29,7 +33,7 @@
     reb_send, reb_recv, reb_sib,
     cov_send, a_own, a_recv, b_own, b_recv, a2_own, a2_send, a2_recv, b2_own, b2_send, b2_recv,
     fin, c3_send, c3_recv,
-    tot_f, tot_b, tot_sib, tot_own, tot_x, x_recv, tot_send, tot_recv,
+    tot_b, tot_sib, tot_own, tot_x, x_recv, tot_send, tot_recv,
     load_sem, z_ss, z_rs, r_ss, r_rs, f_ss, f_rs, s_ss, s_rs,
     a_ss, a_rs, b_ss, b_rs, a2_ss, a2_rs, b2_ss, b2_rs, c3_ss, c3_rs,
     ts_ss, ts_rs, tx_ss, tx_rs, t_ss, t_rs,
@@ -119,7 +123,7 @@
         )
 
     def ts_copy(g):
-        return remote(tot_b.at[g, 1 - core], tot_sib.at[g], ts_ss.at[g], ts_rs.at[g], sibling, sub)
+        return remote(tot_b.at[g], tot_sib.at[g], ts_ss.at[g], ts_rs.at[g], sibling, sub)
 
     def tx_copy(zz):
         return remote(tot_x.at[zz], x_recv.at[zz], tx_ss.at[zz], tx_rs.at[zz], across, sub)
@@ -131,10 +135,10 @@
         )
 
     def owner(t):
-        return (xl + t) % 2 * 4 + (y + t // 2) % 4
+        return (xl + t + 1) % 2 * 4 + (y + (t + 1) // 2) % 4
 
     def origin(t):
-        return (xl + t) % 2 * 4 + (y + 8 - t // 2) % 4
+        return (xl + t + 1) % 2 * 4 + (y + 8 - (t + 1) // 2) % 4
 
     loads[0].wait()
     loads[1].wait()
@@ -151,7 +155,7 @@
             z_send[m] = rotated_t[half * S:(half + 1) * S]
 
     pl.semaphore_wait(barrier, 7 + 7 + 2 + 1)
-    for t in range(1, 4):
+    for t in range(3):
         z_copy(origin(t), sub).start()
     z_recv[sub] = z_send[sub]
 
@@ -162,15 +166,20 @@
                 run * 32:(run + 1) * 32
             ]
     s_copy().start()
-    for t in range(4, 6):
+    for t in range(3, 5):
         z_copy(origin(t), sub).start()
 
     loads[2].wait()
     lane = lax.broadcasted_iota(jnp.int32, (KC, S), 1)
 
+    def source(j, b):
+        half = (xh + 1 + j // 4) % 2
+        parity = (core + 1 + j // 2) % 2
+        return pl.ds(pl.multiple_of(((half * 8 + (z + 1 + j % 2 * 4 + b) % 8) * 2 + parity) * 128, 128), 128)
+
     def prepare(j, carry):
         rows = pl.ds(pl.multiple_of(j * KC, KC), KC)
-        code = codes[rows, :]
+        code = jnp.concatenate([codes[source(j, b), :] for b in range(4)], 0)
         code_f = code.astype(F32)
         bias = -0.5 * jnp.sum(code_f * code_f, axis=1, keepdims=True)
         high = bias.astype(BF).astype(F32)
@@ -186,7 +195,7 @@
         return carry
 
     lax.fori_loop(0, K // KC // 2, prepare, 0)
-    for t in range(6, SUBS):
+    for t in range(5, SUBS - 1):
         z_copy(origin(t), sub).start()
     lax.fori_loop(K // KC // 2, K // KC, prepare, 0)
 
@@ -220,7 +229,7 @@
     def forward(t):
         m = origin(t)
 
-        @pl.when(t != 0)
+        @pl.when(t != SUBS - 1)
         def _():
             r_copy(sub, m).wait_recv()
 
@@ -288,7 +297,8 @@
         b2_own[...] = gather_b(0)[1]
         a2_own[...] = gather_a(0)[1]
 
-    z0 = jnp.concatenate([z_recv[sub], ones], 0)
+    z_copy(sub, owner(0)).wait_recv()
+    z0 = jnp.concatenate([z_recv[owner(0)], ones], 0)
     top = low_start
     for j in range(K // KC):
         top = first(z0, j, logits_a, top)
@@ -299,7 +309,7 @@
             t = tt * 2 + half
             cols = pl.ds(pl.multiple_of(t * ROWS, ROWS), ROWS)
 
-            @pl.when(t < SUBS - 1)
+            @pl.when(t < SUBS - 2)
             def _():
                 z_copy(sub, owner(t + 1)).wait_recv()
 
@@ -311,11 +321,11 @@
                 top = first(z_next, j, logits[1 - half], top)
             who, rebuilt = finish(t, cols, acc)
 
-            @pl.when(t == 0)
+            @pl.when(t == SUBS - 1)
             def _():
                 reb_recv[sub] = rebuilt
 
-            @pl.when(t != 0)
+            @pl.when(t != SUBS - 1)
             def _():
                 reb_send[who] = rebuilt
                 r_copy(who, sub).start()
@@ -332,81 +342,69 @@
 
     lax.fori_loop(0, SUBS // 2, two_steps, top)
 
-    def group(j):
-        return (xh + 1 + j // 4) % 2 * 4 + (z // 2 + 1 + j) % 4
-
     def sums(j):
-        g = group(j)
         value = lax.dot_general(
-            weights[pl.ds(pl.multiple_of(g * TC, TC), TC), :], zl[...], NT, preferred_element_type=F32
-        )
-        for h in range(2):
-            for p in range(2):
-                block = value[(h * 2 + p) * 128:(h * 2 + p + 1) * 128]
-                counts = block[:, S:].T
-                tot_f[g, p, h, :S] = block[:, :S]
-                tot_f[g, p, h, S:] = counts
-                tot_b[g, p, h, :S] = block[:, :S].astype(BF)
-                tot_b[g, p, h, S:] = counts.astype(BF)
-        ts_copy(g).start()
-
-    def pair_sum(j):
-        g = group(j)
-        ts_copy(g).wait_recv()
-        return g, [tot_f[g, core, h] + tot_sib[g, h].astype(F32) for h in range(2)]
-
-    def share_x(j):
-        g, both = pair_sum(j)
-        for h in range(2):
-            zz = g % 4 * 2 + h
-            tot_x[zz] = both[h].astype(BF)
-            tx_copy(zz).start()
-
-    def share_z(j):
-        g, both = pair_sum(j)
-        for h in range(2):
-            zz = g % 4 * 2 + h
-            tx_copy(zz).wait_recv()
-            four = both[h] + x_recv[zz].astype(F32)
-
-            @pl.when(zz == z)
-            def _():
-                tot_own[...] = four
-
-            @pl.when(zz != z)
-            def _():
-                tot_send[zz] = four.astype(BF)
-                t_copy(zz, z).start()
-
-    def sums_step(j, carry):
-        sums(j)
-
-        @pl.when(j < LAG_F)
-        def _():
-            forward(SUBS - LAG_F + j)
-
-        @pl.when(j < LAG_C)
-        def _():
-            cross(SUBS - LAG_C + j)
-
-        @pl.when((j >= 2) & (j < 6))
-        def _():
-            share_x(j - 2)
-
-        @pl.when(j >= 6)
-        def _():
-            share_z(j - 2)
-
-        @pl.when((j % 2 == 0) & (j >= 2))
-        def _():
-            spread_a(j // 2)
-
-        return carry
-
-    lax.fori_loop(0, 8, sums_step, 0)
-    spread_b()
-    share_z(6)
-    share_z(7)
+            weights[j * TC:(j + 1) * TC, :], zl[...], NT, preferred_element_type=F32
+        )
+        return [
+            jnp.concatenate([value[b * 128:b * 128 + 128, :S], value[b * 128:b * 128 + 128, S:].T], 0)
+            for b in range(4)
+        ]
+
+    for j in range(8):
+        pieces = sums(j)
+        pair = j // 4 * 2 + j % 2
+        if j // 2 % 2 == 0:
+            for b in range(4):
+                tot_b[pair, b] = pieces[b].astype(BF)
+            ts_copy(pair).start()
+        else:
+            ts_copy(pair).wait_recv()
+            if j >= 4:
+                tx_copy(j % 2).wait_recv()
+            for b in range(4):
+                piece = pieces[b] + tot_sib[pair, b].astype(F32)
+                if j < 4:
+                    tot_x[j % 2, b] = piece.astype(BF)
+                    continue
+                piece = piece + x_recv[j % 2, b].astype(F32)
+                if (j, b) == (7, 3):
+                    tot_own[...] = piece
+                else:
+                    zz = (z + 1 + j % 2 * 4 + b) % 8
+                    tot_send[zz] = piece.astype(BF)
+                    t_copy(zz, z).start()
+            if j < 4:
+                tx_copy(j % 2).start()
+        for step in FORWARDS.get(j, ()):
+            forward(step)
+        for step in CROSSES.get(j, ()):
+            cross(step)
+        for step in SPREADS.get(j, ()):
+            spread_a(step)
+        if j == SPREAD_B:
+            spread_b()
+    if SPREAD_B == 8:
+        spread_b()
+
+    def sent_sub(j, carry):
+        other = (sub + j) % SUBS
+        z_copy(other, sub).wait_send()
+        r_copy(other, sub).wait_send()
+        f_copy(other).wait_send()
+        return carry
+
+    def sent_ring(j, carry):
+        for ym in range(4):
+            a_copy((x + j) % 4, ym, x).wait_send()
+        for xm in range(2):
+            b_copy((y + j) % 4, xm, y).wait_send()
+        return carry
+
+    lax.fori_loop(1, SUBS, sent_sub, 0)
+    f_copy(sub).wait_send()
+    s_copy().wait_send()
+    lax.fori_loop(1, 4, sent_ring, 0)
 
     acc = a2_own[...]
     for k in range(1, 4):
@@ -437,45 +435,30 @@
     mine = codes[pl.ds(pl.multiple_of(item * 128, 128), 128), :].astype(F32)
     fresh_ref[0] = (total[:S] + mine) / count
 
+    def sent_z(j, carry):
+        t_copy((z + j) % 8, z).wait_send()
+        return carry
+
+    def sent_c(j, carry):
+        c3_copy((z + j) % 8, z).wait_send()
+        return carry
+
+    lax.fori_loop(1, 8, sent_z, 0)
+    for j in range(1, 4):
+        a2_copy((y + j) % 4, y).wait_send()
+        b2_copy((x + j) % 4, x).wait_send()
+    for j in range(4):
+        ts_copy(j).wait_send()
+    for j in range(2):
+        tx_copy(j).wait_send()
+
     def gather_c(j, acc):
         src = (z + j) % 8
         c3_copy(z, src).wait_recv()
         return acc + c3_recv[src].astype(F32)
 
     cross_ref[...] = lax.fori_loop(1, 8, gather_c, fin[pl.ds(pl.multiple_of(z * 32, 32), 32), :])
-
-    def sent_sub(j, carry):
-        other = (sub + j) % SUBS
-        z_copy(other, sub).wait_send()
-        r_copy(other, sub).wait_send()
-        return carry
-
-    def sent_all(j, carry):
-        f_copy(j).wait_send()
-        ts_copy(j).wait_send()
-        tx_copy(j).wait_send()
-        return carry
-
-    def sent_z(j, carry):
-        other = (z + j) % 8
-        t_copy(other, z).wait_send()
-        c3_copy(other, z).wait_send()
-        return carry
-
-    def sent_ring(j, carry):
-        for ym in range(4):
-            a_copy((x + j) % 4, ym, x).wait_send()
-        for xm in range(2):
-            b_copy((y + j) % 4, xm, y).wait_send()
-        a2_copy((y + j) % 4, y).wait_send()
-        b2_copy((x + j) % 4, x).wait_send()
-        return carry
-
-    lax.fori_loop(1, SUBS, sent_sub, 0)
-    lax.fori_loop(0, SUBS, sent_all, 0)
-    lax.fori_loop(1, 8, sent_z, 0)
-    lax.fori_loop(1, 4, sent_ring, 0)
-    s_copy().wait_send()
+    lax.fori_loop(1, 8, sent_c, 0)
 
 
 def body(samples, rotation, codebook):
@@ -519,12 +502,11 @@
             pltpu.VMEM((256, S), F32),
             pltpu.VMEM((8, 32, S), BF),
             pltpu.VMEM((8, 32, S), BF),
-            pltpu.VMEM((8, 2, 2, EXT, S), F32),
-            pltpu.VMEM((8, 2, 2, EXT, S), BF),
-            pltpu.VMEM((8, 2, EXT, S), BF),
+            pltpu.VMEM((4, 4, EXT, S), BF),
+            pltpu.VMEM((4, 4, EXT, S), BF),
             pltpu.VMEM((EXT, S), F32),
-            pltpu.VMEM((8, EXT, S), BF),
-            pltpu.VMEM((8, EXT, S), BF),
+            pltpu.VMEM((2, 4, EXT, S), BF),
+            pltpu.VMEM((2, 4, EXT, S), BF),
             pltpu.VMEM((8, EXT, S), BF),
             pltpu.VMEM((8, EXT, S), BF),
             dma((3,)),

time: 56.5 us -> 55.1 us (0.975)
  the two profiles are of different devices: /device:TPU:30 before, /device:TPU:8 now
where the time goes in v3:
time: 55.1 us; the launch traced here: 54.2 us
  Pallas kernels  50.7 us (92%)
  local copies, waits for them, and re-layouts  2.8 us (5%)
  between operations  0.64 us (1%)
    pallas_call x1, Pallas kernels, body(): pl.pallas_call(kernel, out_shape=(jax.ShapeDtypeStruct((1, 128, S), F32),...  50.7 us
    unnamed x2, local copies, waits for them, and re-layouts  2.8 us

profile of v3, /device:TPU:8, one launch (start us, length us, event | category | flops | bytes accessed | tf_op | source)
XLA Modules:
  0.0 54.2 jit_solution(3835711427470465798)
XLA Ops:
  0.6 50.7 %quantize.1 = (f32[1,128,128]{2,1,0:T(8,128)}, f32[32,128]{1,0:T(8,128)}) custom-call(bf16[256,1024]{1,0:T(8,128)(2,1)} %samples_hbm.1, bf16[1024,1024]{1,0:T(8,128)(2,1)} %rotation_hbm.1, bf16[1,4096,128]{2,1,0:T(8,128)(2,1)} %codebook_hbm.1), custom_call_target="tpu_custom_call" | custom-call | flops 8000000000 | bytes 4194304 | tf_op jit(solution)/shard_map/quantize/pallas_call | solution.py:466
  51.4 1.5 %copy.7 = f32[1,128,128]{2,1,0:T(8,128)} copy(f32[1,128,128]{2,1,0:T(8,128)} %get-tuple-element.4) | data formatting | bytes 131072
  52.8 1.3 %copy.8 = f32[32,128]{1,0:T(8,128)} copy(f32[32,128]{1,0:T(8,128)} %get-tuple-element.5) | data formatting | bytes 32768
